TPU v7x, 512 devices: a whole 4x4x16 slice. The times are simulated.
512 devices in a mesh: grp: 16 (over y, x), dev: 32 (over z, core).
Axes of the slice: x: 4, y: 4, z: 16, core: 2. Of those that a mesh axis runs over, the one named last changes fastest.
Arguments:
- positions: float32 [3, 524288], P(None, ('grp', 'dev')), may hold values from -6 to 6
- velocities: float32 [3, 524288], P(None, ('grp', 'dev')), may hold values from -6 to 6
- masses: float32 [524288], P(('grp', 'dev')), may hold values from 0.2 to 5
- active_index: int32 [1024], replicated, may hold values from 0 to 524287, as said below
Outputs:
- force: float32 [3, 1024], P(None, ('grp', 'dev'))
- jerk: float32 [3, 1024], P(None, ('grp', 'dev'))
Inputs may be any that keep to these rules, and one draw needn't show every extreme that they name: `active_index`: strictly increasing, distinct indices of stars; at most 4 of them fall in any aligned block of 1024 consecutive stars, and some block holds exactly 4.
All inputs are finite; a program needn't handle non-finite values.
Results may differ from a plain program's by a relative error of at most 0.0003.
Values sent between devices are 32-bit elements; how exact they have to be, the bound alone decides.
No kernel may reach another device: no remote copies, remote signals or barrier semaphores. Data moves between devices by JAX's collectives and lax.ppermute only.
A program may use at most 64 MiB of HBM per device.

v0:
```python
import jax
import jax.numpy as jnp
from jax import lax
from jax.sharding import Mesh
from jax.sharding import PartitionSpec as P

GRP = ("grp_0", "grp_1")
DEV = ("dev_0", "dev_1")
GRP_DEV = ("grp_0", "grp_1", "dev_0", "dev_1")


SOFT = 0.0025


def copy_for_each(value, axis):
    copies = jnp.broadcast_to(value, (lax.axis_size(axis), *value.shape))
    return lax.all_to_all(copies, axis, split_axis=0, concat_axis=0, tiled=True)


def laid_out(pieces, dim):
    pieces = jnp.moveaxis(pieces, 0, dim)
    dims = pieces.shape
    return pieces.reshape(*dims[:dim], dims[dim] * dims[dim + 1], *dims[dim + 2 :])


def gathered_by_axis(value, axes, dim):
    far, near = axes
    first = copy_for_each(value, far)
    pieces = jnp.swapaxes(copy_for_each(first, near), 0, 1)
    return laid_out(pieces.reshape(-1, *value.shape), dim)


def in_blocks(value, dim, count):
    dims = value.shape
    pieces = value.reshape(*dims[:dim], count, dims[dim] // count, *dims[dim + 1 :])
    return jnp.moveaxis(pieces, dim, 0)


def summed_on_arrival(value, axis, dim):
    count = lax.axis_size(axis)
    pieces = lax.all_to_all(in_blocks(value, dim, count), axis, 0, 0, tiled=True)
    return jnp.sum(pieces, axis=0)


def sum_in_two_steps(value, axes, dim):
    far, near = axes
    pieces = in_blocks(value, dim, lax.axis_size(far))
    nearer = summed_on_arrival(pieces, near, dim + 1)
    arrived = lax.all_to_all(nearer, far, split_axis=0, concat_axis=0, tiled=True)
    return arrived.sum(axis=0)


def in_one_piece(arrays, axis, dim, along):
    ends, at = ([], 0)
    for a in arrays[:-1]:
        at += a.shape[along]
        ends.append(at)
    both = jnp.concatenate(arrays, axis=along)
    return tuple(jnp.split(sum_in_two_steps(both, axis, dim), ends, axis=along))


def pair_terms(act_pos, act_vel, pos, vel, mass):
    dx = pos[:, None, :] - act_pos[:, :, None]
    dv = vel[:, None, :] - act_vel[:, :, None]
    r2 = jnp.sum(dx * dx, axis=0) + SOFT
    inv = 1.0 / jnp.sqrt(r2)
    weight = mass[None, :] * inv * inv * inv
    rv = jnp.sum(dx * dv, axis=0)
    acc = jnp.sum(weight[None] * dx, axis=-1)
    jer = jnp.sum(weight[None] * dv - (3.0 * rv * weight / r2)[None] * dx, axis=-1)
    return (acc, jer)


def per_device(positions, velocities, masses, active_index):
    local_count = positions.shape[1]
    groups = lax.axis_size(GRP)
    members = lax.axis_size(DEV)
    devices = groups * members
    active = active_index.shape[0]
    owner = lax.axis_index(GRP) * members + lax.axis_index(DEV)
    offset = owner * local_count
    capacity = 2 * active // devices
    starts = jnp.sum(
        (
            active_index[None, :] < (jnp.arange(devices, dtype=jnp.int32) * local_count)[:, None]
        ).astype(jnp.int32),
        axis=1,
    )
    first = jnp.sum((active_index < offset).astype(jnp.int32))
    slots = first + jnp.arange(capacity, dtype=jnp.int32)
    inside = slots < active
    local = jnp.take(active_index, jnp.clip(slots, 0, active - 1)) - offset
    valid = inside & (local >= 0) & (local < local_count)
    clipped = jnp.clip(local, 0, local_count - 1)
    packed = jnp.concatenate(
        [jnp.take(positions, clipped, axis=1), jnp.take(velocities, clipped, axis=1)], axis=0
    )
    packed = jnp.where(valid[None, :], packed, 0.0)
    gathered = gathered_by_axis(packed, (("grp_0", "grp_1"), ("dev_0", "dev_1")), 1)
    holder = active_index // local_count
    place = holder * capacity + jnp.arange(active, dtype=jnp.int32) - jnp.take(starts, holder)
    state = jnp.take(gathered, place, axis=1)
    block = min(256, active)
    nblk = active // block
    blocks = state.reshape(6, nblk, block).transpose(1, 0, 2)

    def one_block(item):
        return pair_terms(item[0:3], item[3:6], positions, velocities, masses)

    acc, jer = lax.map(one_block, blocks)
    scale = 1.0 / (local_count * groups * members)
    acc = acc.transpose(1, 0, 2).reshape(3, active) * scale
    jer = jer.transpose(1, 0, 2).reshape(3, active) * scale
    force, jerk = in_one_piece((acc, jer), (("grp_0", "grp_1"), ("dev_0", "dev_1")), 1, 0)
    return (force, jerk)


def solution(mesh):
    finer = Mesh(mesh.devices.reshape(4, 4, 16, 2), ("grp_0", "grp_1", "dev_0", "dev_1"))
    in_specs = (P(None, GRP_DEV), P(None, GRP_DEV), P(GRP_DEV), P())
    out_specs = (P(None, GRP_DEV), P(None, GRP_DEV))
    return jax.shard_map(
        per_device, mesh=finer, in_specs=in_specs, out_specs=out_specs, check_vma=False
    )
```

profile of v0, /device:TPU:1, one launch (start us, length us, event | category | flops | bytes accessed | tf_op | source)
XLA Modules:
  0.0 100.0 jit_solution(16368683850826318750)
XLA Ops:
  0.7 1.4 %fusion.7 = (s32[1024]{0:T(1024)S(1)}, s32[]{:T(128)}) fusion(s32[1024]{0:T(1024)} %param.11, s32[]{:T(128)S(6)} %mul.132), kind=kLoop, calls=%fused_computation.39 | loop fusion | flops 22527 | bytes 8200 | tf_op jit(solution)/shard_map/jit(_take)/gather | solution.py:101
  2.0 0.7 fusion.8
  2.7 1.3 %gather_fusion.1 = s32[4]{0:T(128)S(1)} fusion(s32[1024]{0:T(1024)} %param.11, s32[1024]{0:T(1024)S(1)} %pad_clamp_fusion.1), kind=kCustom, calls=%fused_computation.3 | custom fusion | bytes 48 | tf_op jit(solution)/shard_map/jit(_take)/gather | solution.py:92
  4.0 0.7 compare_and_fusion.2
  4.7 0.9 copy.62
  7.8 7.6 %all-to-all-start = ((f32[16,6,4]{1,2,0:T(4,128)}), f32[16,6,4]{1,2,0:T(4,128)S(1)}, u32[]{:S(2)}, u32[]{:S(2)}) async-start(f32[16,6,4]{1,2,0:T(4,128)} %broadcast_in_dim.72), calls=%async_computation | async-start | bytes 65536 | tf_op jit(solution)/shard_map/all_to_all | solution.py:17
  15.8 6.9 %gather_fusion = s32[1024]{0:T(1024)S(1)} fusion(s32[512]{0:T(512)S(1)} %convert_reduce_fusion, s32[1024]{0:T(1024)S(1)} %get-tuple-element.73), kind=kCustom, calls=%fused_computation.2 | custom fusion | bytes 12288 | tf_op jit(solution)/shard_map/jit(_take)/gather | solution.py:101
  22.9 0.9 reshape.196
  23.8 16.5 %all-to-all-start.1 = ((f32[32,1,384]{2,1,0:T(1,128)}), f32[32,1,384]{2,1,0:T(1,128)S(1)}, u32[]{:S(2)}, u32[]{:S(2)}) async-start(f32[32,1,384]{2,1,0:T(1,128)} %reshape.196), calls=%async_computation.1 | async-start | bytes 98304 | tf_op jit(solution)/shard_map/all_to_all | solution.py:17
  40.3 12.5 %all-to-all-done.1 = f32[32,1,384]{2,1,0:T(1,128)S(1)} async-done(((f32[32,1,384]{2,1,0:T(1,128)}), f32[32,1,384]{2,1,0:T(1,128)S(1)}, u32[]{:S(2)}, u32[]{:S(2)}) %all-to-all-start.1) | async-done | bytes 49184 | tf_op jit(solution)/shard_map/all_to_all | solution.py:17
  53.3 0.8 reduce
  55.2 2.8 %gather_fusion.2 = f32[1024,6]{1,0:T(8,128)S(1)} fusion(f32[6,2048]{0,1:T(8,128)S(1)} %bitcast.49, s32[1024]{0:T(1024)S(1)} %broadcast_clamp_fusion), kind=kCustom, calls=%fused_computation.4 | custom fusion | bytes 53248 | tf_op jit(solution)/shard_map/jit(_take)/gather | solution.py:102
  58.2 10.1 %while.12 = (s32[]{:T(128)}, f32[4,3,256]{2,1,0:T(4,128)S(1)}, f32[4,3,256]{2,1,0:T(4,128)S(1)}, f32[3,1024]{1,0:T(4,128)S(1)}, f32[4,6,256]{2,1,0:T(8,128)S(1)}...) while((s32[]{:T(128)}, f32[4,3,256]{2,1,0:T(4,128)S(1)}, ...), condition=%wide.region_7.9_spmd, body=%wide.region_2.8_spmd.sunk | while | flops 12319235 | bytes 8489085 | solution.py:110
  58.2 0.7 fusion.14
  59.3 1.5 %fusion.15 = (f32[3,256]{1,0:T(4,128)S(1)}, f32[3,256]{1,0:T(4,128)S(1)}) fusion(f32[256,1024]{1,0:T(8,128)S(1)} %get-tuple-element.138, f32[3,256]{1,0:T(4,128)S(1)} %get-tuple-element.134, f32[3,1024]{1,0:T(4,128)S(1)} %get-tuple-element.170, f32[256,1024]{1,0:T(8,128)S(1)} %get-tuple-element.139, f32[3,256]{1,0:T(4,128)S(1)} %get-tuple-element.135, ...), kind=kLoop, calls=%fused_computation.11.clone.1 | loop fusion | flops 6289920 | bytes 2134016 | tf_op jit(solution)/shard_map/while/body/eval_jaxpr/reduce_sum | solution.py:70
  60.8 0.7 fusion.14
  61.8 1.5 %fusion.15 = (f32[3,256]{1,0:T(4,128)S(1)}, f32[3,256]{1,0:T(4,128)S(1)}) fusion(f32[256,1024]{1,0:T(8,128)S(1)} %get-tuple-element.138, f32[3,256]{1,0:T(4,128)S(1)} %get-tuple-element.134, f32[3,1024]{1,0:T(4,128)S(1)} %get-tuple-element.170, f32[256,1024]{1,0:T(8,128)S(1)} %get-tuple-element.139, f32[3,256]{1,0:T(4,128)S(1)} %get-tuple-element.135, ...), kind=kLoop, calls=%fused_computation.11.clone.1 | loop fusion | flops 6289920 | bytes 2134016 | tf_op jit(solution)/shard_map/while/body/eval_jaxpr/reduce_sum | solution.py:70
  63.3 0.7 fusion.14
  64.3 1.5 %fusion.15 = (f32[3,256]{1,0:T(4,128)S(1)}, f32[3,256]{1,0:T(4,128)S(1)}) fusion(f32[256,1024]{1,0:T(8,128)S(1)} %get-tuple-element.138, f32[3,256]{1,0:T(4,128)S(1)} %get-tuple-element.134, f32[3,1024]{1,0:T(4,128)S(1)} %get-tuple-element.170, f32[256,1024]{1,0:T(8,128)S(1)} %get-tuple-element.139, f32[3,256]{1,0:T(4,128)S(1)} %get-tuple-element.135, ...), kind=kLoop, calls=%fused_computation.11.clone.1 | loop fusion | flops 6289920 | bytes 2134016 | tf_op jit(solution)/shard_map/while/body/eval_jaxpr/reduce_sum | solution.py:70
  65.8 0.7 fusion.14
  66.8 1.5 %fusion.15 = (f32[3,256]{1,0:T(4,128)S(1)}, f32[3,256]{1,0:T(4,128)S(1)}) fusion(f32[256,1024]{1,0:T(8,128)S(1)} %get-tuple-element.138, f32[3,256]{1,0:T(4,128)S(1)} %get-tuple-element.134, f32[3,1024]{1,0:T(4,128)S(1)} %get-tuple-element.170, f32[256,1024]{1,0:T(8,128)S(1)} %get-tuple-element.139, f32[3,256]{1,0:T(4,128)S(1)} %get-tuple-element.135, ...), kind=kLoop, calls=%fused_computation.11.clone.1 | loop fusion | flops 6289920 | bytes 2134016 | tf_op jit(solution)/shard_map/while/body/eval_jaxpr/reduce_sum | solution.py:70
  69.0 16.3 %all_to_all.20 = f32[32,1,192]{2,1,0:T(1,128)S(1)} all-to-all(f32[32,1,192]{2,1,0:T(1,128)S(1)} %reshape.198), channel_id=1, replica_groups=mesh['grp_0'=4,'grp_1'=4,'dev_0'=16,'dev_1'=2] {'dev_0','dev_1'}, dimensions={0} | all-to-all | bytes 49152 | tf_op jit(solution)/shard_map/all_to_all | solution.py:41
  85.3 0.7 reduce.1
  86.4 12.9 %all_to_all.21 = f32[16,6,2]{1,2,0:T(2,128)S(1)} all-to-all(f32[16,6,2]{1,2,0:T(2,128)S(1)} %copy.73), channel_id=1, replica_groups=mesh['grp_0'=4,'grp_1'=4,'dev_0'=16,'dev_1'=2] {'grp_0','grp_1'}, dimensions={0} | all-to-all | bytes 1536 | tf_op jit(solution)/shard_map/all_to_all | solution.py:49
  (61 shorter events, 7.5 us)
Async XLA Ops:
  0.6 14.8 %copy-start = (s32[1024]{0:T(1024)S(1)}, s32[1024]{0:T(1024)}, u32[]{:S(2)}) copy-start(s32[1024]{0:T(1024)} %param.11) | copy-start | bytes 12292
  0.6 5.0 %copy-start.2 = (f32[3,1024]{1,0:T(4,128)S(1)}, f32[3,1024]{1,0:T(4,128)}, u32[]{:S(2)}) copy-start(f32[3,1024]{1,0:T(4,128)} %param.9) | copy-start | bytes 36868
  7.8 14.9 %all-to-all-start = ((f32[16,6,4]{1,2,0:T(4,128)}), f32[16,6,4]{1,2,0:T(4,128)S(1)}, u32[]{:S(2)}, u32[]{:S(2)}) async-start(f32[16,6,4]{1,2,0:T(4,128)} %broadcast_in_dim.72), calls=%async_computation | async-start | bytes 65536 | tf_op jit(solution)/shard_map/all_to_all | solution.py:17
  23.8 29.0 %all-to-all-start.1 = ((f32[32,1,384]{2,1,0:T(1,128)}), f32[32,1,384]{2,1,0:T(1,128)S(1)}, u32[]{:S(2)}, u32[]{:S(2)}) async-start(f32[32,1,384]{2,1,0:T(1,128)} %reshape.196), calls=%async_computation.1 | async-start | bytes 98304 | tf_op jit(solution)/shard_map/all_to_all | solution.py:17
  54.7 3.5 %copy-start.1 = (f32[3,1024]{1,0:T(4,128)S(1)}, f32[3,1024]{1,0:T(4,128)}, u32[]{:S(2)}) copy-start(f32[3,1024]{1,0:T(4,128)} %param.8) | copy-start | bytes 36868
  54.7 3.5 %copy-start.3 = (f32[1024]{0:T(1024)S(1)}, f32[1024]{0:T(1024)}, u32[]{:S(2)}) copy-start(f32[1024]{0:T(1024)} %param.10) | copy-start | bytes 12292
where the time goes:
time: 100 us
  blocking collectives  29.2 us (29%)
  starting transfers between devices  24.1 us (24%)
  local copies, waits for them, and re-layouts  18.4 us (18%)
  other arithmetic  14.7 us (15%)
  waiting for transfers between devices  12.5 us (12%)
    all_to_all x2, starting transfers between devices, copy_for_each(): return lax.all_to_all(copies, axis, split_axis=0, concat_axis=0, tiled=True)  24.1 us
    all_to_all x1, blocking collectives, summed_on_arrival(): lax.all_to_all(in_blocks(value, dim, count), axis, 0, 0, tiled=True)  16.3 us
    all_to_all x1, blocking collectives, sum_in_two_steps(): lax.all_to_all(nearer, far, split_axis=0, concat_axis=0, tiled=True)  12.9 us
    all_to_all x2, waiting for transfers between devices, copy_for_each(): return lax.all_to_all(copies, axis, split_axis=0, concat_axis=0, tiled=True)  12.5 us
    gather x1, local copies, waits for them, and re-layouts, per_device(): jnp.take(starts, holder)  6.87 us
    reduce_sum x4, other arithmetic, pair_terms(): jnp.sum(weight[None] * dv - (3.0 * rv * weight / r2)[None] * dx, axis=-1)  5.84 us
    gather x2, local copies, waits for them, and re-layouts, per_device(): state = jnp.take(gathered, place, axis=1)  3 us
    unnamed x15, local copies, waits for them, and re-layouts  2.89 us
  transfers between devices with their start and end apart: 2, of which 1 were waited for; matrix products, arithmetic and copies ran while one was open for 7% of the time, Pallas kernels for 0%

commit v1 on v0

v1 whole, which is shorter than its diff:
```python
import jax
import jax.numpy as jnp
from jax import lax
from jax.experimental import pallas as pl
from jax.experimental.pallas import tpu as pltpu
from jax.sharding import PartitionSpec as P

SOFT = 0.0025
LANES = 128
WHOLE = pl.BlockSpec(memory_space=pltpu.VMEM)
SCALARS = pl.BlockSpec(memory_space=pltpu.SMEM)


def pack_kernel(index_ref, pos_ref, vel_ref, mass_ref, out_ref):
    active = index_ref.shape[0]
    count = pos_ref.shape[1]
    groups = out_ref.shape[0]
    per_group = active // groups
    owner = lax.axis_index("grp") * lax.axis_size("dev") + lax.axis_index("dev")
    offset = owner * count
    mass = mass_ref[...]
    rows = jnp.concatenate([pos_ref[...], vel_ref[...], mass, jnp.zeros_like(mass)], axis=0)
    for g in range(groups):
        out_ref[g] = rows
    first = jnp.int32(0)
    step = active // 2
    while step:
        first = first + jnp.where(index_ref[first + (step - 1)] < offset, step, 0)
        step //= 2
    first = first + jnp.where(index_ref[first] < offset, 1, 0)
    lane = lax.broadcasted_iota(jnp.int32, (3, LANES), 1)
    for k in range(4):
        rank = jnp.minimum(first + k, active - 1)
        local = index_ref[rank] - offset

        @pl.when((first + k < active) & (local < count))
        def _():
            chunk = pl.ds(pl.multiple_of(local // LANES * LANES, LANES), LANES)
            here = lane == local % LANES
            pos = jnp.sum(jnp.where(here, pos_ref[:, chunk], 0.0), axis=1, keepdims=True)
            vel = jnp.sum(jnp.where(here, vel_ref[:, chunk], 0.0), axis=1, keepdims=True)
            group = rank // per_group
            slot = rank % per_group
            state = jnp.where(lane == slot, pos, jnp.where(lane == slot + LANES // 2, vel, 0.0))
            for c in range(3):
                tile = pl.ds(c * LANES, LANES)
                out_ref[group, 7:8, tile] = out_ref[group, 7:8, tile] + state[c : c + 1]


def spread_kernel(in_ref, out_ref):
    for c in range(3):
        tile = pl.ds(c * LANES, LANES)
        total = in_ref[0, 7:8, tile]
        for g in range(1, in_ref.shape[0]):
            total = total + in_ref[g, 7:8, tile]
        for d in range(out_ref.shape[0]):
            out_ref[d, c] = total


def pairs_kernel(state_ref, field_ref, out_ref):
    sources, _, count = field_ref.shape
    width = 4
    rows = []
    for c in range(3):
        total = state_ref[0, c]
        for d in range(1, state_ref.shape[0]):
            total = total + state_ref[d, c]
        rows.append(total)
    packed = jnp.concatenate(rows + [jnp.zeros((5, LANES), jnp.float32)], axis=0).T
    lane = lax.broadcasted_iota(jnp.int32, (8, LANES), 1)
    half = LANES // 2
    zero = jnp.zeros((8, LANES), jnp.float32)
    for top in range(0, half // 8, width):
        states = [
            [
                jnp.broadcast_to(packed[h + 8 * (top + i) : h + 8 * (top + i) + 8, c : c + 1], (8, LANES))
                for h in (0, half)
                for c in range(3)
            ]
            for i in range(width)
        ]

        def one_source(b, sums, states=states):
            sums = [list(s) for s in sums]
            for t in range(0, count, LANES):
                star = [jnp.broadcast_to(field_ref[b, c : c + 1, t : t + LANES], (8, LANES)) for c in range(7)]
                for act, s in zip(states, sums):
                    dx = [star[c] - act[c] for c in range(3)]
                    dv = [star[3 + c] - act[3 + c] for c in range(3)]
                    r2 = dx[0] * dx[0] + dx[1] * dx[1] + dx[2] * dx[2] + SOFT
                    inv = lax.rsqrt(r2)
                    rv = dx[0] * dv[0] + dx[1] * dv[1] + dx[2] * dv[2]
                    inv2 = inv * inv
                    weight = star[6] * inv * inv2
                    ratio = rv * inv2
                    for c in range(3):
                        pull = weight * dx[c]
                        s[c] = s[c] + pull
                        s[3 + c] = s[3 + c] + weight * dv[c]
                        s[6 + c] = s[6 + c] + ratio * pull
            return tuple(tuple(s) for s in sums)

        sums = lax.fori_loop(0, sources, one_source, ((zero,) * 9,) * width)
        for i, s in enumerate(sums):
            result = zero
            for c in range(3):
                force = jnp.sum(s[c], axis=1, keepdims=True)
                jerk = jnp.sum(s[3 + c] - 3.0 * s[6 + c], axis=1, keepdims=True)
                result = jnp.where(lane == c, force, jnp.where(lane == 3 + c, jerk, result))
            out_ref[pl.ds(8 * (top + i), 8), 0, :] = result


def finish_kernel(scale, in_ref, force_ref, jerk_ref):
    slots = force_ref.shape[0]
    rows = []
    for i in range(slots):
        total = in_ref[i]
        for d in range(1, in_ref.shape[0] // slots):
            total = total + in_ref[d * slots + i]
        rows.append(total)
    rows.append(jnp.zeros((8 - slots, LANES), jnp.float32))
    total = jnp.concatenate(rows, axis=0) * scale
    force_ref[...] = total[0:slots, 0:3]
    jerk_ref[...] = total[0:slots, 3:6]


def per_device(positions, velocities, masses, active_index):
    groups, members = lax.axis_size("grp"), lax.axis_size("dev")
    count = positions.shape[1]
    active = active_index.shape[0]
    f32 = jnp.float32
    packed = pl.pallas_call(
        pack_kernel,
        out_shape=jax.ShapeDtypeStruct((groups, 8, count), f32),
        in_specs=[SCALARS, WHOLE, WHOLE, WHOLE],
        out_specs=WHOLE,
        name="pack",
    )(active_index, positions, velocities, masses.reshape(1, count))
    field = lax.all_to_all(packed, "grp", 0, 0, tiled=True)
    spread = pl.pallas_call(
        spread_kernel,
        out_shape=jax.ShapeDtypeStruct((members, 3, 1, LANES), f32),
        grid=(1,),
        in_specs=[pl.BlockSpec((groups, 8, 3 * LANES), lambda i: (0, 0, 0))],
        out_specs=pl.BlockSpec((members, 3, 1, LANES), lambda i: (0, 0, 0, 0)),
        name="spread",
    )(field)
    states = lax.all_to_all(spread, "dev", 0, 0, tiled=True)
    per_group = active // groups
    partial = pl.pallas_call(
        pairs_kernel,
        out_shape=jax.ShapeDtypeStruct((per_group, 1, LANES), f32),
        in_specs=[WHOLE, WHOLE],
        out_specs=WHOLE,
        name="pairs",
    )(states, field)
    arrived = lax.all_to_all(partial, "dev", 0, 0, tiled=True)
    slots = per_group // members
    out = jax.ShapeDtypeStruct((slots, 3), f32)
    scale = 1.0 / (count * groups * members)
    force, jerk = pl.pallas_call(
        lambda *refs: finish_kernel(scale, *refs),
        out_shape=(out, out),
        in_specs=[WHOLE],
        out_specs=(WHOLE, WHOLE),
        name="finish",
    )(arrived)
    return force.T, jerk.T


def solution(mesh):
    both = ("grp", "dev")
    return jax.shard_map(
        per_device,
        mesh=mesh,
        in_specs=(P(None, both), P(None, both), P(both), P()),
        out_specs=(P(None, both), P(None, both)),
        check_vma=False,
    )
```

time: 100 us -> 79.8 us (0.80)
  blocking collectives: 29.2 us -> 65.9 us
  starting transfers between devices: 24.1 us -> 0 us
  local copies, waits for them, and re-layouts: 18.4 us -> 0 us
  other arithmetic: 14.7 us -> 0 us
  Pallas kernels: 0 us -> 12.8 us
  waiting for transfers between devices: 12.5 us -> 0 us
    all_to_all x2 -> x3, blocking collectives: 29.2 us -> 65.9 us  [the longest x1 31.1 us: per_device(): states = lax.all_to_all(spread, 'dev', 0, 0, tiled=True)]
    all_to_all x2 -> x0, starting transfers between devices: 24.1 us -> none  [copy_for_each(): return lax.all_to_all(copies, axis, split_axis=0, concat_axis=0, tiled=True)]
    pallas_call x0 -> x4, Pallas kernels: none -> 12.8 us  [the longest x1 8.04 us: per_device(): pl.pallas_call(pairs_kernel, out_shape=jax.ShapeDtypeStruct((per_group, 1...]
    all_to_all x2 -> x0, waiting for transfers between devices: 12.5 us -> none  [copy_for_each(): return lax.all_to_all(copies, axis, split_axis=0, concat_axis=0, tiled=True)]
    gather x6 -> x0, local copies, waits for them, and re-layouts: 12.3 us -> none  [the longest x1 6.87 us: per_device(): jnp.take(starts, holder)]
    reduce_sum x11 -> x0, other arithmetic: 9.01 us -> none  [the longest x4 5.84 us: pair_terms(): jnp.sum(weight[None] * dv - (3.0 * rv * weight / r2)[None] * dx, axis=-1)]
    unnamed x15 -> x0, local copies, waits for them, and re-layouts: 2.89 us -> none
    all_to_all x2 -> x0, other arithmetic: 1.48 us -> none  [the longest x1 0.76 us: copy_for_each(): return lax.all_to_all(copies, axis, split_axis=0, concat_axis=0, tiled=True)]
  transfers between devices with their start and end apart: 2 -> 0, of which waited for: 1 -> 0; matrix products, arithmetic and copies ran while one was open for 7% -> 0% of each run, Pallas kernels for 0% -> 0%
where the time goes in v1:
time: 79.8 us; the launch traced here: 79.4 us
  blocking collectives  65.9 us (83%)
  Pallas kernels  12.8 us (16%)
    all_to_all x1, blocking collectives, per_device(): states = lax.all_to_all(spread, 'dev', 0, 0, tiled=True)  31.1 us
    all_to_all x1, blocking collectives, per_device(): arrived = lax.all_to_all(partial, 'dev', 0, 0, tiled=True)  17.9 us
    all_to_all x1, blocking collectives, per_device(): field = lax.all_to_all(packed, 'grp', 0, 0, tiled=True)  16.9 us
    pallas_call x1, Pallas kernels, per_device(): pl.pallas_call(pairs_kernel, out_shape=jax.ShapeDtypeStruct((per_group, 1...  8.04 us
    pallas_call x1, Pallas kernels, per_device(): pl.pallas_call(pack_kernel, out_shape=jax.ShapeDtypeStruct((groups, 8, co...  1.79 us

profile of v1, /device:TPU:1, one launch (start us, length us, event | category | flops | bytes accessed | tf_op | source)
XLA Modules:
  0.0 79.4 jit_solution(12277010694469092387)
XLA Ops:
  0.6 1.8 %pack.1 = f32[16,8,1024]{2,1,0:T(8,128)} custom-call(s32[1024]{0:T(1024)} %index_ref.1, f32[3,1024]{1,0:T(4,128)} %pos_ref.1, f32[3,1024]{1,0:T(4,128)} %vel_ref.1, f32[1,1024]{1,0:T(1,128)} %bitcast.3), custom_call_target="tpu_custom_call" | custom-call | tf_op jit(solution)/shard_map/pack/pallas_call | solution.py:132
  2.4 16.9 %all_to_all.15.in_ref.field_ref = f32[16,8,1024]{2,1,0:T(8,128)} all-to-all(f32[16,8,1024]{2,1,0:T(8,128)} %pack.1), channel_id=1, replica_groups=mesh['grp'=16,'dev'=32] {'grp'}, dimensions={0} | all-to-all | bytes 1048576 | tf_op jit(solution)/shard_map/all_to_all | solution.py:139
  19.4 1.6 %spread.1 = f32[32,3,1,128]{3,2,1,0:T(1,128)} custom-call(f32[16,8,1024]{2,1,0:T(8,128)} %all_to_all.15.in_ref.field_ref), custom_call_target="tpu_custom_call" | custom-call | tf_op jit(solution)/shard_map/spread/pallas_call | solution.py:140
  21.0 31.1 %all_to_all.16.state_ref = f32[32,3,1,128]{3,2,1,0:T(1,128)} all-to-all(f32[32,3,1,128]{3,2,1,0:T(1,128)} %spread.1), channel_id=1, replica_groups=mesh['grp'=16,'dev'=32] {'dev'}, dimensions={0} | all-to-all | bytes 98304 | tf_op jit(solution)/shard_map/all_to_all | solution.py:148
  52.0 8.0 %pairs.1 = f32[64,1,128]{2,1,0:T(1,128)} custom-call(f32[32,3,1,128]{3,2,1,0:T(1,128)} %all_to_all.16.state_ref, f32[16,8,1024]{2,1,0:T(8,128)} %all_to_all.15.in_ref.field_ref), custom_call_target="tpu_custom_call" | custom-call | tf_op jit(solution)/shard_map/pairs/pallas_call | solution.py:150
  60.1 17.9 %all_to_all.17.refs_0_ = f32[64,1,128]{2,1,0:T(1,128)} all-to-all(f32[64,1,128]{2,1,0:T(1,128)} %pairs.1), channel_id=1, replica_groups=mesh['grp'=16,'dev'=32] {'dev'}, dimensions={0} | all-to-all | bytes 65536 | tf_op jit(solution)/shard_map/all_to_all | solution.py:157
  77.9 1.4 %finish.1 = (f32[2,3]{1,0:T(2,128)}, f32[2,3]{1,0:T(2,128)}) custom-call(f32[64,1,128]{2,1,0:T(1,128)} %all_to_all.17.refs_0_), custom_call_target="tpu_custom_call" | custom-call | tf_op jit(solution)/shard_map/finish/pallas_call | solution.py:161

commit v2 on v1

--- a/solution.py
+++ b/solution.py
@@ -41,6 +41,7 @@
             vel = jnp.sum(jnp.where(here, vel_ref[:, chunk], 0.0), axis=1, keepdims=True)
             group = rank // per_group
             slot = rank % per_group
+            slot = slot % 2 * (per_group // 2) + slot // 2
             state = jnp.where(lane == slot, pos, jnp.where(lane == slot + LANES // 2, vel, 0.0))
             for c in range(3):
                 tile = pl.ds(c * LANES, LANES)
@@ -70,6 +71,7 @@
     lane = lax.broadcasted_iota(jnp.int32, (8, LANES), 1)
     half = LANES // 2
     zero = jnp.zeros((8, LANES), jnp.float32)
+    results = []
     for top in range(0, half // 8, width):
         states = [
             [
@@ -101,27 +103,30 @@
             return tuple(tuple(s) for s in sums)
 
         sums = lax.fori_loop(0, sources, one_source, ((zero,) * 9,) * width)
-        for i, s in enumerate(sums):
+        first = 6 * (2 * top // (half // 8))
+        for s in sums:
             result = zero
             for c in range(3):
                 force = jnp.sum(s[c], axis=1, keepdims=True)
                 jerk = jnp.sum(s[3 + c] - 3.0 * s[6 + c], axis=1, keepdims=True)
-                result = jnp.where(lane == c, force, jnp.where(lane == 3 + c, jerk, result))
-            out_ref[pl.ds(8 * (top + i), 8), 0, :] = result
+                result = jnp.where(lane == first + c, force, jnp.where(lane == first + 3 + c, jerk, result))
+            results.append(result)
+    for i in range(len(results) // 2):
+        out_ref[pl.ds(8 * i, 8), 0, :] = results[i] + results[i + len(results) // 2]
 
 
 def finish_kernel(scale, in_ref, force_ref, jerk_ref):
-    slots = force_ref.shape[0]
-    rows = []
-    for i in range(slots):
-        total = in_ref[i]
-        for d in range(1, in_ref.shape[0] // slots):
-            total = total + in_ref[d * slots + i]
-        rows.append(total)
-    rows.append(jnp.zeros((8 - slots, LANES), jnp.float32))
-    total = jnp.concatenate(rows, axis=0) * scale
-    force_ref[...] = total[0:slots, 0:3]
-    jerk_ref[...] = total[0:slots, 3:6]
+    total = in_ref[0]
+    for d in range(1, in_ref.shape[0]):
+        total = total + in_ref[d]
+    total = total * scale
+    for slot in range(force_ref.shape[0]):
+        force_ref[slot : slot + 1, :] = total[:, 6 * slot : 6 * slot + 3]
+        jerk_ref[slot : slot + 1, :] = total[:, 6 * slot + 3 : 6 * slot + 6]
+
+
+def near(x):
+    return pltpu.with_memory_space_constraint(x, pltpu.VMEM)
 
 
 def per_device(positions, velocities, masses, active_index):
@@ -131,7 +136,7 @@
     f32 = jnp.float32
     packed = pl.pallas_call(
         pack_kernel,
-        out_shape=jax.ShapeDtypeStruct((groups, 8, count), f32),
+        out_shape=pltpu.VMEM((groups, 8, count), f32),
         in_specs=[SCALARS, WHOLE, WHOLE, WHOLE],
         out_specs=WHOLE,
         name="pack",
@@ -139,21 +144,20 @@
     field = lax.all_to_all(packed, "grp", 0, 0, tiled=True)
     spread = pl.pallas_call(
         spread_kernel,
-        out_shape=jax.ShapeDtypeStruct((members, 3, 1, LANES), f32),
-        grid=(1,),
-        in_specs=[pl.BlockSpec((groups, 8, 3 * LANES), lambda i: (0, 0, 0))],
-        out_specs=pl.BlockSpec((members, 3, 1, LANES), lambda i: (0, 0, 0, 0)),
+        out_shape=pltpu.VMEM((members, 3, 1, LANES), f32),
+        in_specs=[WHOLE],
+        out_specs=WHOLE,
         name="spread",
-    )(field)
+    )(near(field))
     states = lax.all_to_all(spread, "dev", 0, 0, tiled=True)
     per_group = active // groups
     partial = pl.pallas_call(
         pairs_kernel,
-        out_shape=jax.ShapeDtypeStruct((per_group, 1, LANES), f32),
+        out_shape=pltpu.VMEM((members, 1, LANES), f32),
         in_specs=[WHOLE, WHOLE],
         out_specs=WHOLE,
         name="pairs",
-    )(states, field)
+    )(near(states), near(field))
     arrived = lax.all_to_all(partial, "dev", 0, 0, tiled=True)
     slots = per_group // members
     out = jax.ShapeDtypeStruct((slots, 3), f32)
@@ -164,7 +168,7 @@
         in_specs=[WHOLE],
         out_specs=(WHOLE, WHOLE),
         name="finish",
-    )(arrived)
+    )(near(arrived))
     return force.T, jerk.T
 
 

time: 79.8 us -> 72.5 us (0.909)
  Pallas kernels: 12.8 us -> 8.19 us
  blocking collectives: 65.9 us -> 63.4 us
    pallas_call x3, Pallas kernels: 11.4 us -> 7.52 us  [the longest x1 6.36 us: per_device(): pl.pallas_call(pairs_kernel, out_shape=pltpu.VMEM((members, 1, LANES), f3...]
    all_to_all x1, blocking collectives: 17.9 us -> 16 us  [per_device(): arrived = lax.all_to_all(partial, 'dev', 0, 0, tiled=True)]
where the time goes in v2:
time: 72.5 us; the launch traced here: 72.2 us
  blocking collectives  63.4 us (87%)
  Pallas kernels  8.19 us (11%)
    all_to_all x1, blocking collectives, per_device(): states = lax.all_to_all(spread, 'dev', 0, 0, tiled=True)  30.6 us
    all_to_all x1, blocking collectives, per_device(): field = lax.all_to_all(packed, 'grp', 0, 0, tiled=True)  16.8 us
    all_to_all x1, blocking collectives, per_device(): arrived = lax.all_to_all(partial, 'dev', 0, 0, tiled=True)  16 us
    pallas_call x1, Pallas kernels, per_device(): pl.pallas_call(pairs_kernel, out_shape=pltpu.VMEM((members, 1, LANES), f3...  6.36 us

profile of v2, /device:TPU:1, one launch (start us, length us, event | category | flops | bytes accessed | tf_op | source)
XLA Modules:
  0.0 72.2 jit_solution(1124913799574775620)
XLA Ops:
  0.6 1.1 %pack.1 = f32[16,8,1024]{2,1,0:T(8,128)S(1)} custom-call(s32[1024]{0:T(1024)} %index_ref.1, f32[3,1024]{1,0:T(4,128)} %pos_ref.1, f32[3,1024]{1,0:T(4,128)} %vel_ref.1, f32[1,1024]{1,0:T(1,128)} %bitcast.3), custom_call_target="tpu_custom_call" | custom-call | tf_op jit(solution)/shard_map/pack/pallas_call | solution.py:137
  1.8 16.8 %all_to_all.15.in_ref.field_ref = f32[16,8,1024]{2,1,0:T(8,128)S(1)} all-to-all(f32[16,8,1024]{2,1,0:T(8,128)S(1)} %pack.1), channel_id=1, replica_groups=mesh['grp'=16,'dev'=32] {'grp'}, dimensions={0} | all-to-all | bytes 1048576 | tf_op jit(solution)/shard_map/all_to_all | solution.py:144
  18.6 30.6 %all_to_all.16.state_ref = f32[32,3,1,128]{3,2,1,0:T(1,128)S(1)} all-to-all(f32[32,3,1,128]{3,2,1,0:T(1,128)S(1)} %spread.1), channel_id=1, replica_groups=mesh['grp'=16,'dev'=32] {'dev'}, dimensions={0} | all-to-all | bytes 98304 | tf_op jit(solution)/shard_map/all_to_all | solution.py:152
  49.2 6.4 %pairs.1 = f32[32,1,128]{2,1,0:T(1,128)S(1)} custom-call(f32[32,3,1,128]{3,2,1,0:T(1,128)S(1)} %all_to_all.16.state_ref, f32[16,8,1024]{2,1,0:T(8,128)S(1)} %all_to_all.15.in_ref.field_ref), custom_call_target="tpu_custom_call" | custom-call | tf_op jit(solution)/shard_map/pairs/pallas_call | solution.py:154
  55.6 16.0 %all_to_all.17.refs_0_ = f32[32,1,128]{2,1,0:T(1,128)S(1)} all-to-all(f32[32,1,128]{2,1,0:T(1,128)S(1)} %pairs.1), channel_id=1, replica_groups=mesh['grp'=16,'dev'=32] {'dev'}, dimensions={0} | all-to-all | bytes 32768 | tf_op jit(solution)/shard_map/all_to_all | solution.py:161
  71.5 0.7 finish.1
  (1 shorter events, 0.0 us)

commit v3 on v2

--- a/solution.py
+++ b/solution.py
@@ -7,6 +7,8 @@
 
 SOFT = 0.0025
 LANES = 128
+GRP_FIRST = 10
+DEV_FIRST = 16
 WHOLE = pl.BlockSpec(memory_space=pltpu.VMEM)
 SCALARS = pl.BlockSpec(memory_space=pltpu.SMEM)
 
@@ -39,13 +41,13 @@
             here = lane == local % LANES
             pos = jnp.sum(jnp.where(here, pos_ref[:, chunk], 0.0), axis=1, keepdims=True)
             vel = jnp.sum(jnp.where(here, vel_ref[:, chunk], 0.0), axis=1, keepdims=True)
-            group = rank // per_group
+            row = (rank // per_group + (groups - GRP_FIRST)) % groups
             slot = rank % per_group
             slot = slot % 2 * (per_group // 2) + slot // 2
             state = jnp.where(lane == slot, pos, jnp.where(lane == slot + LANES // 2, vel, 0.0))
             for c in range(3):
                 tile = pl.ds(c * LANES, LANES)
-                out_ref[group, 7:8, tile] = out_ref[group, 7:8, tile] + state[c : c + 1]
+                out_ref[row, 7:8, tile] = out_ref[row, 7:8, tile] + state[c : c + 1]
 
 
 def spread_kernel(in_ref, out_ref):
@@ -111,8 +113,10 @@
                 jerk = jnp.sum(s[3 + c] - 3.0 * s[6 + c], axis=1, keepdims=True)
                 result = jnp.where(lane == first + c, force, jnp.where(lane == first + 3 + c, jerk, result))
             results.append(result)
+    members = out_ref.shape[0]
     for i in range(len(results) // 2):
-        out_ref[pl.ds(8 * i, 8), 0, :] = results[i] + results[i + len(results) // 2]
+        row = (8 * i + members - DEV_FIRST) % members
+        out_ref[pl.ds(row, 8), 0, :] = results[i] + results[i + len(results) // 2]
 
 
 def finish_kernel(scale, in_ref, force_ref, jerk_ref):
@@ -123,6 +127,12 @@
     for slot in range(force_ref.shape[0]):
         force_ref[slot : slot + 1, :] = total[:, 6 * slot : 6 * slot + 3]
         jerk_ref[slot : slot + 1, :] = total[:, 6 * slot + 3 : 6 * slot + 6]
+
+
+def exchanged(x, axis, first):
+    count = lax.axis_size(axis)
+    order = [(first + m) % count for m in range(count)]
+    return lax.all_to_all(x, axis, 0, 0, axis_index_groups=[order], tiled=True)
 
 
 def near(x):
@@ -141,7 +151,7 @@
         out_specs=WHOLE,
         name="pack",
     )(active_index, positions, velocities, masses.reshape(1, count))
-    field = lax.all_to_all(packed, "grp", 0, 0, tiled=True)
+    field = exchanged(packed, "grp", GRP_FIRST)
     spread = pl.pallas_call(
         spread_kernel,
         out_shape=pltpu.VMEM((members, 3, 1, LANES), f32),
@@ -149,7 +159,7 @@
         out_specs=WHOLE,
         name="spread",
     )(near(field))
-    states = lax.all_to_all(spread, "dev", 0, 0, tiled=True)
+    states = exchanged(spread, "dev", DEV_FIRST)
     per_group = active // groups
     partial = pl.pallas_call(
         pairs_kernel,
@@ -158,7 +168,7 @@
         out_specs=WHOLE,
         name="pairs",
     )(near(states), near(field))
-    arrived = lax.all_to_all(partial, "dev", 0, 0, tiled=True)
+    arrived = exchanged(partial, "dev", DEV_FIRST)
     slots = per_group // members
     out = jax.ShapeDtypeStruct((slots, 3), f32)
     scale = 1.0 / (count * groups * members)

time: 72.5 us -> 63 us (0.87)
  blocking collectives: 63.4 us -> 53.9 us
    all_to_all x3, blocking collectives: 63.4 us -> 53.9 us  [exchanged(): return lax.all_to_all(x, axis, 0, 0, axis_index_groups=[order], tiled=True)]
where the time goes in v3:
time: 63 us; the launch traced here: 62.7 us
  blocking collectives  53.9 us (86%)
  Pallas kernels  8.19 us (13%)
  between operations  0.64 us (1%)
    all_to_all x3, blocking collectives, exchanged(): return lax.all_to_all(x, axis, 0, 0, axis_index_groups=[order], tiled=True)  53.9 us
    pallas_call x1, Pallas kernels, per_device(): pl.pallas_call(pairs_kernel, out_shape=pltpu.VMEM((members, 1, LANES), f3...  6.36 us

profile of v3, /device:TPU:1, one launch (start us, length us, event | category | flops | bytes accessed | tf_op | source)
XLA Modules:
  0.0 62.7 jit_solution(11610475627802315106)
XLA Ops:
  0.6 1.1 %pack.1 = f32[16,8,1024]{2,1,0:T(8,128)S(1)} custom-call(s32[1024]{0:T(1024)} %index_ref.1, f32[3,1024]{1,0:T(4,128)} %pos_ref.1, f32[3,1024]{1,0:T(4,128)} %vel_ref.1, f32[1,1024]{1,0:T(1,128)} %bitcast.3), custom_call_target="tpu_custom_call" | custom-call | tf_op jit(solution)/shard_map/pack/pallas_call | solution.py:147
  1.7 13.3 %all_to_all.15.in_ref.field_ref = f32[16,8,1024]{2,1,0:T(8,128)S(1)} all-to-all(f32[16,8,1024]{2,1,0:T(8,128)S(1)} %pack.1), channel_id=1, replica_groups={{320,352,384,416,448,480,0,32,64,96,128,160,192,224,256,288},{321,353,3..., dimensions={0} | all-to-all | bytes 1048576 | tf_op jit(solution)/shard_map/all_to_all | solution.py:135
  15.1 25.4 %all_to_all.16.state_ref = f32[32,3,1,128]{3,2,1,0:T(1,128)S(1)} all-to-all(f32[32,3,1,128]{3,2,1,0:T(1,128)S(1)} %spread.1), channel_id=1, replica_groups={{16,17,18,19,20,21,22,23,24,25,26,27,28,29,30,31,0,1,2,3,4,5,6,7,8,9,10..., dimensions={0} | all-to-all | bytes 98304 | tf_op jit(solution)/shard_map/all_to_all | solution.py:135
  40.5 6.4 %pairs.1 = f32[32,1,128]{2,1,0:T(1,128)S(1)} custom-call(f32[32,3,1,128]{3,2,1,0:T(1,128)S(1)} %all_to_all.16.state_ref, f32[16,8,1024]{2,1,0:T(8,128)S(1)} %all_to_all.15.in_ref.field_ref), custom_call_target="tpu_custom_call" | custom-call | tf_op jit(solution)/shard_map/pairs/pallas_call | solution.py:164
  46.9 15.1 %all_to_all.17.refs_0_ = f32[32,1,128]{2,1,0:T(1,128)S(1)} all-to-all(f32[32,1,128]{2,1,0:T(1,128)S(1)} %pairs.1), channel_id=1, replica_groups={{16,17,18,19,20,21,22,23,24,25,26,27,28,29,30,31,0,1,2,3,4,5,6,7,8,9,10..., dimensions={0} | all-to-all | bytes 32768 | tf_op jit(solution)/shard_map/all_to_all | solution.py:135
  62.0 0.7 %finish.1 = (f32[2,3]{1,0:T(2,128)}, f32[2,3]{1,0:T(2,128)}) custom-call(f32[32,1,128]{2,1,0:T(1,128)S(1)} %all_to_all.17.refs_0_), custom_call_target="tpu_custom_call" | custom-call | tf_op jit(solution)/shard_map/finish/pallas_call | solution.py:175
  (1 shorter events, 0.0 us)

commit v4 on v2

--- a/solution.py
+++ b/solution.py
@@ -7,8 +7,22 @@
 
 SOFT = 0.0025
 LANES = 128
+YX = (4, 4)
+ZC = (16, 2)
 WHOLE = pl.BlockSpec(memory_space=pltpu.VMEM)
 SCALARS = pl.BlockSpec(memory_space=pltpu.SMEM)
+
+
+def turned(index, dims):
+    major, minor = dims
+    first = (index // minor + major // 2) % major
+    second = (index % minor + (minor // 2 if minor > 2 else 0)) % minor
+    return second * major + first
+
+
+def exchanged(x, axis, dims):
+    order = sorted(range(dims[0] * dims[1]), key=lambda index: turned(index, dims))
+    return lax.all_to_all(x, axis, 0, 0, axis_index_groups=[order], tiled=True)
 
 
 def pack_kernel(index_ref, pos_ref, vel_ref, mass_ref, out_ref):
@@ -39,13 +53,13 @@
             here = lane == local % LANES
             pos = jnp.sum(jnp.where(here, pos_ref[:, chunk], 0.0), axis=1, keepdims=True)
             vel = jnp.sum(jnp.where(here, vel_ref[:, chunk], 0.0), axis=1, keepdims=True)
-            group = rank // per_group
+            row = turned(rank // per_group, YX)
             slot = rank % per_group
-            slot = slot % 2 * (per_group // 2) + slot // 2
+            slot = slot % 2 * (per_group // 2) + turned(slot // 2, ZC)
             state = jnp.where(lane == slot, pos, jnp.where(lane == slot + LANES // 2, vel, 0.0))
             for c in range(3):
                 tile = pl.ds(c * LANES, LANES)
-                out_ref[group, 7:8, tile] = out_ref[group, 7:8, tile] + state[c : c + 1]
+                out_ref[row, 7:8, tile] = out_ref[row, 7:8, tile] + state[c : c + 1]
 
 
 def spread_kernel(in_ref, out_ref):
@@ -102,7 +116,7 @@
                         s[6 + c] = s[6 + c] + ratio * pull
             return tuple(tuple(s) for s in sums)
 
-        sums = lax.fori_loop(0, sources, one_source, ((zero,) * 9,) * width)
+        sums = lax.fori_loop(0, sources, one_source, ((zero,) * 9,) * width, unroll=2)
         first = 6 * (2 * top // (half // 8))
         for s in sums:
             result = zero
@@ -141,7 +155,7 @@
         out_specs=WHOLE,
         name="pack",
     )(active_index, positions, velocities, masses.reshape(1, count))
-    field = lax.all_to_all(packed, "grp", 0, 0, tiled=True)
+    field = exchanged(packed, "grp", YX)
     spread = pl.pallas_call(
         spread_kernel,
         out_shape=pltpu.VMEM((members, 3, 1, LANES), f32),
@@ -149,7 +163,7 @@
         out_specs=WHOLE,
         name="spread",
     )(near(field))
-    states = lax.all_to_all(spread, "dev", 0, 0, tiled=True)
+    states = exchanged(spread, "dev", ZC)
     per_group = active // groups
     partial = pl.pallas_call(
         pairs_kernel,
@@ -158,7 +172,7 @@
         out_specs=WHOLE,
         name="pairs",
     )(near(states), near(field))
-    arrived = lax.all_to_all(partial, "dev", 0, 0, tiled=True)
+    arrived = exchanged(partial, "dev", ZC)
     slots = per_group // members
     out = jax.ShapeDtypeStruct((slots, 3), f32)
     scale = 1.0 / (count * groups * members)

time: 72.5 us -> 62.4 us (0.86)
  blocking collectives: 63.4 us -> 53.5 us
    all_to_all x3, blocking collectives: 63.4 us -> 53.5 us  [exchanged(): return lax.all_to_all(x, axis, 0, 0, axis_index_groups=[order], tiled=True)]
where the time goes in v4:
time: 62.4 us; the launch traced here: 62.2 us
  blocking collectives  53.5 us (86%)
  Pallas kernels  8.03 us (13%)
  between operations  0.64 us (1%)
    all_to_all x3, blocking collectives, exchanged(): return lax.all_to_all(x, axis, 0, 0, axis_index_groups=[order], tiled=True)  53.5 us
    pallas_call x1, Pallas kernels, per_device(): pl.pallas_call(pairs_kernel, out_shape=pltpu.VMEM((members, 1, LANES), f3...  6.2 us

profile of v4, /device:TPU:1, one launch (start us, length us, event | category | flops | bytes accessed | tf_op | source)
XLA Modules:
  0.0 62.2 jit_solution(14219885715343144885)
XLA Ops:
  0.6 1.1 %pack.1 = f32[16,8,1024]{2,1,0:T(8,128)S(1)} custom-call(s32[1024]{0:T(1024)} %index_ref.1, f32[3,1024]{1,0:T(4,128)} %pos_ref.1, f32[3,1024]{1,0:T(4,128)} %vel_ref.1, f32[1,1024]{1,0:T(1,128)} %bitcast.3), custom_call_target="tpu_custom_call" | custom-call | tf_op jit(solution)/shard_map/pack/pallas_call | solution.py:151
  1.7 13.4 %all_to_all.15.in_ref.field_ref = f32[16,8,1024]{2,1,0:T(8,128)S(1)} all-to-all(f32[16,8,1024]{2,1,0:T(8,128)S(1)} %pack.1), channel_id=1, replica_groups={{320,448,64,192,352,480,96,224,256,384,0,128,288,416,32,160},{321,449,6..., dimensions={0} | all-to-all | bytes 1048576 | tf_op jit(solution)/shard_map/all_to_all | solution.py:25
  15.2 25.8 %all_to_all.16.state_ref = f32[32,3,1,128]{3,2,1,0:T(1,128)S(1)} all-to-all(f32[32,3,1,128]{3,2,1,0:T(1,128)S(1)} %spread.1), channel_id=1, replica_groups={{16,18,20,22,24,26,28,30,0,2,4,6,8,10,12,14,17,19,21,23,25,27,29,31,1,3..., dimensions={0} | all-to-all | bytes 98304 | tf_op jit(solution)/shard_map/all_to_all | solution.py:25
  41.0 6.2 %pairs.1 = f32[32,1,128]{2,1,0:T(1,128)S(1)} custom-call(f32[32,3,1,128]{3,2,1,0:T(1,128)S(1)} %all_to_all.16.state_ref, f32[16,8,1024]{2,1,0:T(8,128)S(1)} %all_to_all.15.in_ref.field_ref), custom_call_target="tpu_custom_call" | custom-call | tf_op jit(solution)/shard_map/pairs/pallas_call | solution.py:168
  47.2 14.3 %all_to_all.17.refs_0_ = f32[32,1,128]{2,1,0:T(1,128)S(1)} all-to-all(f32[32,1,128]{2,1,0:T(1,128)S(1)} %pairs.1), channel_id=1, replica_groups={{16,18,20,22,24,26,28,30,0,2,4,6,8,10,12,14,17,19,21,23,25,27,29,31,1,3..., dimensions={0} | all-to-all | bytes 32768 | tf_op jit(solution)/shard_map/all_to_all | solution.py:25
  61.5 0.7 %finish.1 = (f32[2,3]{1,0:T(2,128)}, f32[2,3]{1,0:T(2,128)}) custom-call(f32[32,1,128]{2,1,0:T(1,128)S(1)} %all_to_all.17.refs_0_), custom_call_target="tpu_custom_call" | custom-call | tf_op jit(solution)/shard_map/finish/pallas_call | solution.py:179
  (1 shorter events, 0.0 us)

commit v5 on v4

--- a/solution.py
+++ b/solution.py
@@ -72,35 +72,51 @@
             out_ref[d, c] = total
 
 
+def in_parts(x, count):
+    parts = []
+    for _ in range(count):
+        parts.append(x.astype(jnp.bfloat16).astype(jnp.float32))
+        x = x - parts[-1]
+    return parts
+
+
 def pairs_kernel(state_ref, field_ref, out_ref):
     sources, _, count = field_ref.shape
-    width = 4
+    half = LANES // 2
+    f32, bf16 = jnp.float32, jnp.bfloat16
     rows = []
     for c in range(3):
         total = state_ref[0, c]
         for d in range(1, state_ref.shape[0]):
             total = total + state_ref[d, c]
         rows.append(total)
-    packed = jnp.concatenate(rows + [jnp.zeros((5, LANES), jnp.float32)], axis=0).T
-    lane = lax.broadcasted_iota(jnp.int32, (8, LANES), 1)
-    half = LANES // 2
-    zero = jnp.zeros((8, LANES), jnp.float32)
-    results = []
-    for top in range(0, half // 8, width):
-        states = [
+    state = jnp.concatenate(rows + [jnp.zeros((5, LANES), f32)], axis=0)
+    packed = state.T
+    actives = [
+        [jnp.broadcast_to(packed[h + g : h + g + 8, c : c + 1], (8, LANES)) for h in (0, half) for c in range(3)]
+        for g in range(0, half, 8)
+    ]
+    pos0, vel0 = state[0:3, 0:1], state[0:3, half : half + 1]
+    origin = jnp.concatenate([pos0, vel0, jnp.zeros((2, 1), f32)], axis=0)
+    row = lax.broadcasted_iota(jnp.int32, (8, count), 0)
+    step = 2 * LANES
+
+    def one_source(b, sums):
+        stars = jnp.where(row == 6, 1.0, field_ref[b] - origin)
+        high, middle, low = in_parts(stars, 3)
+        stars = jnp.concatenate(
             [
-                jnp.broadcast_to(packed[h + 8 * (top + i) : h + 8 * (top + i) + 8, c : c + 1], (8, LANES))
-                for h in (0, half)
-                for c in range(3)
-            ]
-            for i in range(width)
-        ]
-
-        def one_source(b, sums, states=states):
-            sums = [list(s) for s in sums]
-            for t in range(0, count, LANES):
+                jnp.concatenate([high, middle], axis=0).astype(bf16),
+                jnp.concatenate([low, jnp.zeros_like(low)], axis=0).astype(bf16),
+            ],
+            axis=0,
+        )
+        for start in range(0, count, step):
+            weights, ratios = [], []
+            for t in range(start, start + step, LANES):
                 star = [jnp.broadcast_to(field_ref[b, c : c + 1, t : t + LANES], (8, LANES)) for c in range(7)]
-                for act, s in zip(states, sums):
+                column_w, column_r = [], []
+                for act in actives:
                     dx = [star[c] - act[c] for c in range(3)]
                     dv = [star[3 + c] - act[3 + c] for c in range(3)]
                     r2 = dx[0] * dx[0] + dx[1] * dx[1] + dx[2] * dx[2] + SOFT
@@ -108,25 +124,35 @@
                     rv = dx[0] * dv[0] + dx[1] * dv[1] + dx[2] * dv[2]
                     inv2 = inv * inv
                     weight = star[6] * inv * inv2
-                    ratio = rv * inv2
-                    for c in range(3):
-                        pull = weight * dx[c]
-                        s[c] = s[c] + pull
-                        s[3 + c] = s[3 + c] + weight * dv[c]
-                        s[6 + c] = s[6 + c] + ratio * pull
-            return tuple(tuple(s) for s in sums)
-
-        sums = lax.fori_loop(0, sources, one_source, ((zero,) * 9,) * width, unroll=2)
-        first = 6 * (2 * top // (half // 8))
-        for s in sums:
-            result = zero
-            for c in range(3):
-                force = jnp.sum(s[c], axis=1, keepdims=True)
-                jerk = jnp.sum(s[3 + c] - 3.0 * s[6 + c], axis=1, keepdims=True)
-                result = jnp.where(lane == first + c, force, jnp.where(lane == first + 3 + c, jerk, result))
-            results.append(result)
-    for i in range(len(results) // 2):
-        out_ref[pl.ds(8 * i, 8), 0, :] = results[i] + results[i + len(results) // 2]
+                    column_w.append(weight)
+                    column_r.append(rv * inv2 * weight)
+                weights.append(jnp.concatenate(column_w, axis=0))
+                ratios.append(jnp.concatenate(column_r, axis=0))
+            parts = in_parts(jnp.concatenate(weights, axis=1), 2) + in_parts(jnp.concatenate(ratios, axis=1), 2)
+            sums = sums + lax.dot_general(
+                stars[:, start : start + step],
+                jnp.concatenate([p.astype(bf16) for p in parts], axis=0),
+                (((1,), (1,)), ((), ())),
+                preferred_element_type=f32,
+            )
+        return sums
+
+    sums = jnp.zeros((32, 4 * half), f32)
+    for b in range(sources):
+        sums = one_source(b, sums)
+    sums = sums[0:8] + sums[8:16] + sums[16:24]
+    by_weight, by_ratio = sums[:, :LANES], sums[:, LANES:]
+    by_weight = by_weight + pltpu.roll(by_weight, half, 1)
+    by_ratio = by_ratio + pltpu.roll(by_ratio, half, 1)
+    pos = state[0:3] - pos0
+    vel = pltpu.roll(state, half, 1)[0:3] - vel0
+    force = by_weight[0:3] - pos * by_weight[6:7]
+    jerk = by_weight[3:6] - vel * by_weight[6:7] - 3.0 * (by_ratio[0:3] - pos * by_ratio[6:7])
+    even = jnp.concatenate([force, jerk, jnp.zeros((2, LANES), f32)], axis=0)
+    odd = pltpu.roll(even, LANES - half // 2, 1)
+    out = jnp.concatenate([even[0:6], odd[0:6], jnp.zeros((LANES - 12, LANES), f32)], axis=0).T
+    for i in range(0, half // 2, 8):
+        out_ref[pl.ds(i, 8), 0, :] = out[i : i + 8]
 
 
 def finish_kernel(scale, in_ref, force_ref, jerk_ref):

time: 62.4 us -> 61.2 us (0.981)
  Pallas kernels: 8.03 us -> 6.61 us
    pallas_call x1, Pallas kernels: 6.2 us -> 4.91 us  [per_device(): pl.pallas_call(pairs_kernel, out_shape=pltpu.VMEM((members, 1, LANES), f3...]
where the time goes in v5:
time: 61.2 us; the launch traced here: 60.9 us
  blocking collectives  53.6 us (88%)
  Pallas kernels  6.61 us (11%)
  between operations  0.65 us (1%)
    all_to_all x3, blocking collectives, exchanged(): return lax.all_to_all(x, axis, 0, 0, axis_index_groups=[order], tiled=True)  53.6 us
    pallas_call x1, Pallas kernels, per_device(): pl.pallas_call(pairs_kernel, out_shape=pltpu.VMEM((members, 1, LANES), f3...  4.91 us

profile of v5, /device:TPU:1, one launch (start us, length us, event | category | flops | bytes accessed | tf_op | source)
XLA Modules:
  0.0 60.9 jit_solution(5886109189590801053)
XLA Ops:
  0.6 1.0 %pack.1 = f32[16,8,1024]{2,1,0:T(8,128)S(1)} custom-call(s32[1024]{0:T(1024)} %index_ref.1, f32[3,1024]{1,0:T(4,128)} %pos_ref.1, f32[3,1024]{1,0:T(4,128)} %vel_ref.1, f32[1,1024]{1,0:T(1,128)} %bitcast.3), custom_call_target="tpu_custom_call" | custom-call | tf_op jit(solution)/shard_map/pack/pallas_call | solution.py:177
  1.6 13.5 %all_to_all.15.in_ref.field_ref = f32[16,8,1024]{2,1,0:T(8,128)S(1)} all-to-all(f32[16,8,1024]{2,1,0:T(8,128)S(1)} %pack.1), channel_id=1, replica_groups={{320,448,64,192,352,480,96,224,256,384,0,128,288,416,32,160},{321,449,6..., dimensions={0} | all-to-all | bytes 1048576 | tf_op jit(solution)/shard_map/all_to_all | solution.py:25
  15.2 25.8 %all_to_all.16.state_ref = f32[32,3,1,128]{3,2,1,0:T(1,128)S(1)} all-to-all(f32[32,3,1,128]{3,2,1,0:T(1,128)S(1)} %spread.1), channel_id=1, replica_groups={{16,18,20,22,24,26,28,30,0,2,4,6,8,10,12,14,17,19,21,23,25,27,29,31,1,3..., dimensions={0} | all-to-all | bytes 98304 | tf_op jit(solution)/shard_map/all_to_all | solution.py:25
  41.0 4.9 %pairs.1 = f32[32,1,128]{2,1,0:T(1,128)S(1)} custom-call(f32[32,3,1,128]{3,2,1,0:T(1,128)S(1)} %all_to_all.16.state_ref, f32[16,8,1024]{2,1,0:T(8,128)S(1)} %all_to_all.15.in_ref.field_ref), custom_call_target="tpu_custom_call" | custom-call | tf_op jit(solution)/shard_map/pairs/pallas_call | solution.py:194
  45.9 14.3 %all_to_all.17.refs_0_ = f32[32,1,128]{2,1,0:T(1,128)S(1)} all-to-all(f32[32,1,128]{2,1,0:T(1,128)S(1)} %pairs.1), channel_id=1, replica_groups={{16,18,20,22,24,26,28,30,0,2,4,6,8,10,12,14,17,19,21,23,25,27,29,31,1,3..., dimensions={0} | all-to-all | bytes 32768 | tf_op jit(solution)/shard_map/all_to_all | solution.py:25
  60.2 0.7 %finish.1 = (f32[2,3]{1,0:T(2,128)}, f32[2,3]{1,0:T(2,128)}) custom-call(f32[32,1,128]{2,1,0:T(1,128)S(1)} %all_to_all.17.refs_0_), custom_call_target="tpu_custom_call" | custom-call | tf_op jit(solution)/shard_map/finish/pallas_call | solution.py:205
  (1 shorter events, 0.0 us)

commit v6 on v5

--- a/solution.py
+++ b/solution.py
@@ -7,22 +7,29 @@
 
 SOFT = 0.0025
 LANES = 128
-YX = (4, 4)
-ZC = (16, 2)
+GRP_HEAD = (10, 0)
+DEV_HEAD = (17, 1, 0)
+GRP_ORDER = GRP_HEAD + tuple(
+    g for g in ((2 + i) % 4 * 4 + (2 + j) % 4 for j in range(4) for i in range(4)) if g not in GRP_HEAD
+)
+DEV_ORDER = DEV_HEAD + tuple(
+    d for d in ((8 + i) % 16 * 2 + c for c in (1, 0) for i in range(16)) if d not in DEV_HEAD
+)
 WHOLE = pl.BlockSpec(memory_space=pltpu.VMEM)
 SCALARS = pl.BlockSpec(memory_space=pltpu.SMEM)
 
 
-def turned(index, dims):
-    major, minor = dims
-    first = (index // minor + major // 2) % major
-    second = (index % minor + (minor // 2 if minor > 2 else 0)) % minor
-    return second * major + first
-
-
-def exchanged(x, axis, dims):
-    order = sorted(range(dims[0] * dims[1]), key=lambda index: turned(index, dims))
-    return lax.all_to_all(x, axis, 0, 0, axis_index_groups=[order], tiled=True)
+def place_in(order, index):
+    places = [order.index(i) for i in range(len(order))]
+    words = [sum(p << 8 * n for n, p in enumerate(places[i : i + 4])) for i in range(0, len(places), 4)]
+    word = jnp.int32(words[0])
+    for i in range(1, len(words)):
+        word = jnp.where(index >= 4 * i, words[i], word)
+    return (word >> 8 * (index & 3)) & 255
+
+
+def exchanged(x, axis, order):
+    return lax.all_to_all(x, axis, 0, 0, axis_index_groups=[list(order)], tiled=True)
 
 
 def pack_kernel(index_ref, pos_ref, vel_ref, mass_ref, out_ref):
@@ -43,23 +50,25 @@
         step //= 2
     first = first + jnp.where(index_ref[first] < offset, 1, 0)
     lane = lax.broadcasted_iota(jnp.int32, (3, LANES), 1)
+    rows = []
     for k in range(4):
         rank = jnp.minimum(first + k, active - 1)
         local = index_ref[rank] - offset
-
-        @pl.when((first + k < active) & (local < count))
-        def _():
-            chunk = pl.ds(pl.multiple_of(local // LANES * LANES, LANES), LANES)
-            here = lane == local % LANES
-            pos = jnp.sum(jnp.where(here, pos_ref[:, chunk], 0.0), axis=1, keepdims=True)
-            vel = jnp.sum(jnp.where(here, vel_ref[:, chunk], 0.0), axis=1, keepdims=True)
-            row = turned(rank // per_group, YX)
-            slot = rank % per_group
-            slot = slot % 2 * (per_group // 2) + turned(slot // 2, ZC)
-            state = jnp.where(lane == slot, pos, jnp.where(lane == slot + LANES // 2, vel, 0.0))
-            for c in range(3):
-                tile = pl.ds(c * LANES, LANES)
-                out_ref[row, 7:8, tile] = out_ref[row, 7:8, tile] + state[c : c + 1]
+        held = (first + k < active) & (local < count)
+        local = jnp.clip(local, 0, count - 1)
+        chunk = pl.ds(pl.multiple_of(lax.div(local, LANES) * LANES, LANES), LANES)
+        here = lane == lax.rem(local, LANES)
+        pos = jnp.sum(jnp.where(here, pos_ref[:, chunk], 0.0), axis=1, keepdims=True)
+        vel = jnp.sum(jnp.where(here, vel_ref[:, chunk], 0.0), axis=1, keepdims=True)
+        slot = lax.rem(rank, per_group)
+        slot = (slot & 1) * (per_group // 2) + place_in(DEV_ORDER, slot >> 1)
+        slot = jnp.where(held, slot, LANES)
+        state = jnp.where(lane == slot, pos, jnp.where(lane == slot + LANES // 2, vel, 0.0))
+        rows.append((place_in(GRP_ORDER, lax.div(rank, per_group)), state))
+    for row, state in rows:
+        for c in range(3):
+            tile = pl.ds(c * LANES, LANES)
+            out_ref[row, 7:8, tile] = out_ref[row, 7:8, tile] + state[c : c + 1]
 
 
 def spread_kernel(in_ref, out_ref):
@@ -181,7 +190,7 @@
         out_specs=WHOLE,
         name="pack",
     )(active_index, positions, velocities, masses.reshape(1, count))
-    field = exchanged(packed, "grp", YX)
+    field = exchanged(packed, "grp", GRP_ORDER)
     spread = pl.pallas_call(
         spread_kernel,
         out_shape=pltpu.VMEM((members, 3, 1, LANES), f32),
@@ -189,7 +198,7 @@
         out_specs=WHOLE,
         name="spread",
     )(near(field))
-    states = exchanged(spread, "dev", ZC)
+    states = exchanged(spread, "dev", DEV_ORDER)
     per_group = active // groups
     partial = pl.pallas_call(
         pairs_kernel,
@@ -198,7 +207,7 @@
         out_specs=WHOLE,
         name="pairs",
     )(near(states), near(field))
-    arrived = exchanged(partial, "dev", ZC)
+    arrived = exchanged(partial, "dev", DEV_ORDER)
     slots = per_group // members
     out = jax.ShapeDtypeStruct((slots, 3), f32)
     scale = 1.0 / (count * groups * members)

time: 61.2 us -> 60 us (0.980)
  blocking collectives: 53.6 us -> 52.4 us
    all_to_all x3, blocking collectives: 53.6 us -> 52.4 us  [exchanged(): lax.all_to_all(x, axis, 0, 0, axis_index_groups=[list(order)], tiled=True)]
where the time goes in v6:
time: 60 us; the launch traced here: 59.8 us
  blocking collectives  52.4 us (87%)
  Pallas kernels  6.67 us (11%)
  between operations  0.64 us (1%)
    all_to_all x3, blocking collectives, exchanged(): lax.all_to_all(x, axis, 0, 0, axis_index_groups=[list(order)], tiled=True)  52.4 us
    pallas_call x1, Pallas kernels, per_device(): pl.pallas_call(pairs_kernel, out_shape=pltpu.VMEM((members, 1, LANES), f3...  4.91 us

profile of v6, /device:TPU:1, one launch (start us, length us, event | category | flops | bytes accessed | tf_op | source)
XLA Modules:
  0.0 59.8 jit_solution(3881007075239476403)
XLA Ops:
  0.6 1.0 %pack.1 = f32[16,8,1024]{2,1,0:T(8,128)S(1)} custom-call(s32[1024]{0:T(1024)} %index_ref.1, f32[3,1024]{1,0:T(4,128)} %pos_ref.1, f32[3,1024]{1,0:T(4,128)} %vel_ref.1, f32[1,1024]{1,0:T(1,128)} %bitcast.3), custom_call_target="tpu_custom_call" | custom-call | tf_op jit(solution)/shard_map/pack/pallas_call | solution.py:186
  1.7 13.2 %all_to_all.15.in_ref.field_ref = f32[16,8,1024]{2,1,0:T(8,128)S(1)} all-to-all(f32[16,8,1024]{2,1,0:T(8,128)S(1)} %pack.1), channel_id=1, replica_groups={{320,0,448,64,192,352,480,96,224,256,384,128,288,416,32,160},{321,1,449..., dimensions={0} | all-to-all | bytes 1048576 | tf_op jit(solution)/shard_map/all_to_all | solution.py:32
  14.9 25.3 %all_to_all.16.state_ref = f32[32,3,1,128]{3,2,1,0:T(1,128)S(1)} all-to-all(f32[32,3,1,128]{3,2,1,0:T(1,128)S(1)} %spread.1), channel_id=1, replica_groups={{17,1,0,19,21,23,25,27,29,31,3,5,7,9,11,13,15,16,18,20,22,24,26,28,30,2..., dimensions={0} | all-to-all | bytes 98304 | tf_op jit(solution)/shard_map/all_to_all | solution.py:32
  40.2 4.9 %pairs.1 = f32[32,1,128]{2,1,0:T(1,128)S(1)} custom-call(f32[32,3,1,128]{3,2,1,0:T(1,128)S(1)} %all_to_all.16.state_ref, f32[16,8,1024]{2,1,0:T(8,128)S(1)} %all_to_all.15.in_ref.field_ref), custom_call_target="tpu_custom_call" | custom-call | tf_op jit(solution)/shard_map/pairs/pallas_call | solution.py:203
  45.1 14.0 %all_to_all.17.refs_0_ = f32[32,1,128]{2,1,0:T(1,128)S(1)} all-to-all(f32[32,1,128]{2,1,0:T(1,128)S(1)} %pairs.1), channel_id=1, replica_groups={{17,1,0,19,21,23,25,27,29,31,3,5,7,9,11,13,15,16,18,20,22,24,26,28,30,2..., dimensions={0} | all-to-all | bytes 32768 | tf_op jit(solution)/shard_map/all_to_all | solution.py:32
  59.1 0.7 %finish.1 = (f32[2,3]{1,0:T(2,128)}, f32[2,3]{1,0:T(2,128)}) custom-call(f32[32,1,128]{2,1,0:T(1,128)S(1)} %all_to_all.17.refs_0_), custom_call_target="tpu_custom_call" | custom-call | tf_op jit(solution)/shard_map/finish/pallas_call | solution.py:214
  (1 shorter events, 0.0 us)

commit v7 on v6

--- a/solution.py
+++ b/solution.py
@@ -7,13 +7,13 @@
 
 SOFT = 0.0025
 LANES = 128
-GRP_HEAD = (10, 0)
-DEV_HEAD = (17, 1, 0)
+GRP_HEAD = (10, 0, 8, 2, 12, 3)
+DEV_HEAD = (17,)
 GRP_ORDER = GRP_HEAD + tuple(
     g for g in ((2 + i) % 4 * 4 + (2 + j) % 4 for j in range(4) for i in range(4)) if g not in GRP_HEAD
 )
 DEV_ORDER = DEV_HEAD + tuple(
-    d for d in ((8 + i) % 16 * 2 + c for c in (1, 0) for i in range(16)) if d not in DEV_HEAD
+    d for d in (2 * z + c for z in sorted(range(16), key=lambda z: min(z, 16 - z)) for c in (1, 0)) if d not in DEV_HEAD
 )
 WHOLE = pl.BlockSpec(memory_space=pltpu.VMEM)
 SCALARS = pl.BlockSpec(memory_space=pltpu.SMEM)

time: 60 us -> 59.7 us (level)
  no operation moved by 1% of the time
where the time goes in v7:
time: 59.7 us; the launch traced here: 59.5 us
  blocking collectives  52.1 us (87%)
  Pallas kernels  6.67 us (11%)
  between operations  0.64 us (1%)
    all_to_all x3, blocking collectives, exchanged(): lax.all_to_all(x, axis, 0, 0, axis_index_groups=[list(order)], tiled=True)  52.1 us
    pallas_call x1, Pallas kernels, per_device(): pl.pallas_call(pairs_kernel, out_shape=pltpu.VMEM((members, 1, LANES), f3...  4.91 us

profile of v7, /device:TPU:1, one launch (start us, length us, event | category | flops | bytes accessed | tf_op | source)
XLA Modules:
  0.0 59.5 jit_solution(11180317195091040257)
XLA Ops:
  0.6 1.0 %pack.1 = f32[16,8,1024]{2,1,0:T(8,128)S(1)} custom-call(s32[1024]{0:T(1024)} %index_ref.1, f32[3,1024]{1,0:T(4,128)} %pos_ref.1, f32[3,1024]{1,0:T(4,128)} %vel_ref.1, f32[1,1024]{1,0:T(1,128)} %bitcast.3), custom_call_target="tpu_custom_call" | custom-call | tf_op jit(solution)/shard_map/pack/pallas_call | solution.py:186
  1.7 12.9 %all_to_all.15.in_ref.field_ref = f32[16,8,1024]{2,1,0:T(8,128)S(1)} all-to-all(f32[16,8,1024]{2,1,0:T(8,128)S(1)} %pack.1), channel_id=1, replica_groups={{320,0,256,64,384,96,448,192,352,480,224,128,288,416,32,160},{321,1,257..., dimensions={0} | all-to-all | bytes 1048576 | tf_op jit(solution)/shard_map/all_to_all | solution.py:32
  14.6 25.1 %all_to_all.16.state_ref = f32[32,3,1,128]{3,2,1,0:T(1,128)S(1)} all-to-all(f32[32,3,1,128]{3,2,1,0:T(1,128)S(1)} %spread.1), channel_id=1, replica_groups={{17,1,0,3,2,31,30,5,4,29,28,7,6,27,26,9,8,25,24,11,10,23,22,13,12,21,20..., dimensions={0} | all-to-all | bytes 98304 | tf_op jit(solution)/shard_map/all_to_all | solution.py:32
  39.7 4.9 %pairs.1 = f32[32,1,128]{2,1,0:T(1,128)S(1)} custom-call(f32[32,3,1,128]{3,2,1,0:T(1,128)S(1)} %all_to_all.16.state_ref, f32[16,8,1024]{2,1,0:T(8,128)S(1)} %all_to_all.15.in_ref.field_ref), custom_call_target="tpu_custom_call" | custom-call | tf_op jit(solution)/shard_map/pairs/pallas_call | solution.py:203
  44.7 14.1 %all_to_all.17.refs_0_ = f32[32,1,128]{2,1,0:T(1,128)S(1)} all-to-all(f32[32,1,128]{2,1,0:T(1,128)S(1)} %pairs.1), channel_id=1, replica_groups={{17,1,0,3,2,31,30,5,4,29,28,7,6,27,26,9,8,25,24,11,10,23,22,13,12,21,20..., dimensions={0} | all-to-all | bytes 32768 | tf_op jit(solution)/shard_map/all_to_all | solution.py:32
  58.8 0.7 %finish.1 = (f32[2,3]{1,0:T(2,128)}, f32[2,3]{1,0:T(2,128)}) custom-call(f32[32,1,128]{2,1,0:T(1,128)S(1)} %all_to_all.17.refs_0_), custom_call_target="tpu_custom_call" | custom-call | tf_op jit(solution)/shard_map/finish/pallas_call | solution.py:214
  (1 shorter events, 0.0 us)

commit v8 on v7

--- a/solution.py
+++ b/solution.py
@@ -111,7 +111,8 @@
     step = 2 * LANES
 
     def one_source(b, sums):
-        stars = jnp.where(row == 6, 1.0, field_ref[b] - origin)
+        stars = field_ref[b] - origin
+        stars = jnp.where(row == 6, stars, stars * field_ref[b, 6:7, :])
         high, middle, low = in_parts(stars, 3)
         stars = jnp.concatenate(
             [
@@ -123,7 +124,7 @@
         for start in range(0, count, step):
             weights, ratios = [], []
             for t in range(start, start + step, LANES):
-                star = [jnp.broadcast_to(field_ref[b, c : c + 1, t : t + LANES], (8, LANES)) for c in range(7)]
+                star = [jnp.broadcast_to(field_ref[b, c : c + 1, t : t + LANES], (8, LANES)) for c in range(6)]
                 column_w, column_r = [], []
                 for act in actives:
                     dx = [star[c] - act[c] for c in range(3)]
@@ -132,7 +133,7 @@
                     inv = lax.rsqrt(r2)
                     rv = dx[0] * dv[0] + dx[1] * dv[1] + dx[2] * dv[2]
                     inv2 = inv * inv
-                    weight = star[6] * inv * inv2
+                    weight = inv * inv2
                     column_w.append(weight)
                     column_r.append(rv * inv2 * weight)
                 weights.append(jnp.concatenate(column_w, axis=0))

time: 59.7 us -> 59.6 us (level)
  no operation moved by 1% of the time
where the time goes in v8:
time: 59.6 us; the launch traced here: 59.4 us
  blocking collectives  52.1 us (87%)
  Pallas kernels  6.59 us (11%)
  between operations  0.64 us (1%)
    all_to_all x3, blocking collectives, exchanged(): lax.all_to_all(x, axis, 0, 0, axis_index_groups=[list(order)], tiled=True)  52.1 us
    pallas_call x1, Pallas kernels, per_device(): pl.pallas_call(pairs_kernel, out_shape=pltpu.VMEM((members, 1, LANES), f3...  4.83 us

profile of v8, /device:TPU:1, one launch (start us, length us, event | category | flops | bytes accessed | tf_op | source)
XLA Modules:
  0.0 59.4 jit_solution(7036913688122359740)
XLA Ops:
  0.6 1.0 %pack.1 = f32[16,8,1024]{2,1,0:T(8,128)S(1)} custom-call(s32[1024]{0:T(1024)} %index_ref.1, f32[3,1024]{1,0:T(4,128)} %pos_ref.1, f32[3,1024]{1,0:T(4,128)} %vel_ref.1, f32[1,1024]{1,0:T(1,128)} %bitcast.3), custom_call_target="tpu_custom_call" | custom-call | tf_op jit(solution)/shard_map/pack/pallas_call | solution.py:187
  1.7 12.9 %all_to_all.15.in_ref.field_ref = f32[16,8,1024]{2,1,0:T(8,128)S(1)} all-to-all(f32[16,8,1024]{2,1,0:T(8,128)S(1)} %pack.1), channel_id=1, replica_groups={{320,0,256,64,384,96,448,192,352,480,224,128,288,416,32,160},{321,1,257..., dimensions={0} | all-to-all | bytes 1048576 | tf_op jit(solution)/shard_map/all_to_all | solution.py:32
  14.6 25.1 %all_to_all.16.state_ref = f32[32,3,1,128]{3,2,1,0:T(1,128)S(1)} all-to-all(f32[32,3,1,128]{3,2,1,0:T(1,128)S(1)} %spread.1), channel_id=1, replica_groups={{17,1,0,3,2,31,30,5,4,29,28,7,6,27,26,9,8,25,24,11,10,23,22,13,12,21,20..., dimensions={0} | all-to-all | bytes 98304 | tf_op jit(solution)/shard_map/all_to_all | solution.py:32
  39.7 4.8 %pairs.1 = f32[32,1,128]{2,1,0:T(1,128)S(1)} custom-call(f32[32,3,1,128]{3,2,1,0:T(1,128)S(1)} %all_to_all.16.state_ref, f32[16,8,1024]{2,1,0:T(8,128)S(1)} %all_to_all.15.in_ref.field_ref), custom_call_target="tpu_custom_call" | custom-call | tf_op jit(solution)/shard_map/pairs/pallas_call | solution.py:204
  44.6 14.1 %all_to_all.17.refs_0_ = f32[32,1,128]{2,1,0:T(1,128)S(1)} all-to-all(f32[32,1,128]{2,1,0:T(1,128)S(1)} %pairs.1), channel_id=1, replica_groups={{17,1,0,3,2,31,30,5,4,29,28,7,6,27,26,9,8,25,24,11,10,23,22,13,12,21,20..., dimensions={0} | all-to-all | bytes 32768 | tf_op jit(solution)/shard_map/all_to_all | solution.py:32
  58.7 0.7 %finish.1 = (f32[2,3]{1,0:T(2,128)}, f32[2,3]{1,0:T(2,128)}) custom-call(f32[32,1,128]{2,1,0:T(1,128)S(1)} %all_to_all.17.refs_0_), custom_call_target="tpu_custom_call" | custom-call | tf_op jit(solution)/shard_map/finish/pallas_call | solution.py:215
  (1 shorter events, 0.0 us)

commit v9 on v8

--- a/solution.py
+++ b/solution.py
@@ -7,7 +7,7 @@
 
 SOFT = 0.0025
 LANES = 128
-GRP_HEAD = (10, 0, 8, 2, 12, 3)
+GRP_HEAD = (10, 0, 12, 3, 8, 2)
 DEV_HEAD = (17,)
 GRP_ORDER = GRP_HEAD + tuple(
     g for g in ((2 + i) % 4 * 4 + (2 + j) % 4 for j in range(4) for i in range(4)) if g not in GRP_HEAD

time: 59.6 us -> 59.6 us (level)
  no operation moved by 1% of the time
where the time goes in v9:
time: 59.6 us; the launch traced here: 59.3 us
  blocking collectives  52.1 us (87%)
  Pallas kernels  6.59 us (11%)
  between operations  0.64 us (1%)
    all_to_all x3, blocking collectives, exchanged(): lax.all_to_all(x, axis, 0, 0, axis_index_groups=[list(order)], tiled=True)  52.1 us
    pallas_call x1, Pallas kernels, per_device(): pl.pallas_call(pairs_kernel, out_shape=pltpu.VMEM((members, 1, LANES), f3...  4.83 us

profile of v9, /device:TPU:1, one launch (start us, length us, event | category | flops | bytes accessed | tf_op | source)
XLA Modules:
  0.0 59.3 jit_solution(13195448983500606284)
XLA Ops:
  0.6 1.0 %pack.1 = f32[16,8,1024]{2,1,0:T(8,128)S(1)} custom-call(s32[1024]{0:T(1024)} %index_ref.1, f32[3,1024]{1,0:T(4,128)} %pos_ref.1, f32[3,1024]{1,0:T(4,128)} %vel_ref.1, f32[1,1024]{1,0:T(1,128)} %bitcast.3), custom_call_target="tpu_custom_call" | custom-call | tf_op jit(solution)/shard_map/pack/pallas_call | solution.py:187
  1.7 12.8 %all_to_all.15.in_ref.field_ref = f32[16,8,1024]{2,1,0:T(8,128)S(1)} all-to-all(f32[16,8,1024]{2,1,0:T(8,128)S(1)} %pack.1), channel_id=1, replica_groups={{320,0,384,96,256,64,448,192,352,480,224,128,288,416,32,160},{321,1,385..., dimensions={0} | all-to-all | bytes 1048576 | tf_op jit(solution)/shard_map/all_to_all | solution.py:32
  14.5 25.1 %all_to_all.16.state_ref = f32[32,3,1,128]{3,2,1,0:T(1,128)S(1)} all-to-all(f32[32,3,1,128]{3,2,1,0:T(1,128)S(1)} %spread.1), channel_id=1, replica_groups={{17,1,0,3,2,31,30,5,4,29,28,7,6,27,26,9,8,25,24,11,10,23,22,13,12,21,20..., dimensions={0} | all-to-all | bytes 98304 | tf_op jit(solution)/shard_map/all_to_all | solution.py:32
  39.7 4.8 %pairs.1 = f32[32,1,128]{2,1,0:T(1,128)S(1)} custom-call(f32[32,3,1,128]{3,2,1,0:T(1,128)S(1)} %all_to_all.16.state_ref, f32[16,8,1024]{2,1,0:T(8,128)S(1)} %all_to_all.15.in_ref.field_ref), custom_call_target="tpu_custom_call" | custom-call | tf_op jit(solution)/shard_map/pairs/pallas_call | solution.py:204
  44.5 14.1 %all_to_all.17.refs_0_ = f32[32,1,128]{2,1,0:T(1,128)S(1)} all-to-all(f32[32,1,128]{2,1,0:T(1,128)S(1)} %pairs.1), channel_id=1, replica_groups={{17,1,0,3,2,31,30,5,4,29,28,7,6,27,26,9,8,25,24,11,10,23,22,13,12,21,20..., dimensions={0} | all-to-all | bytes 32768 | tf_op jit(solution)/shard_map/all_to_all | solution.py:32
  58.6 0.7 %finish.1 = (f32[2,3]{1,0:T(2,128)}, f32[2,3]{1,0:T(2,128)}) custom-call(f32[32,1,128]{2,1,0:T(1,128)S(1)} %all_to_all.17.refs_0_), custom_call_target="tpu_custom_call" | custom-call | tf_op jit(solution)/shard_map/finish/pallas_call | solution.py:215
  (1 shorter events, 0.0 us)

commit v10 on v9

--- a/solution.py
+++ b/solution.py
@@ -8,7 +8,7 @@
 SOFT = 0.0025
 LANES = 128
 GRP_HEAD = (10, 0, 12, 3, 8, 2)
-DEV_HEAD = (17,)
+DEV_HEAD = (17, 1, 0, 16)
 GRP_ORDER = GRP_HEAD + tuple(
     g for g in ((2 + i) % 4 * 4 + (2 + j) % 4 for j in range(4) for i in range(4)) if g not in GRP_HEAD
 )

time: 59.6 us -> 59.6 us (level)
  no operation moved by 1% of the time
where the time goes in v10:
time: 59.6 us; the launch traced here: 59.3 us
  blocking collectives  52.1 us (87%)
  Pallas kernels  6.59 us (11%)
  between operations  0.64 us (1%)
    all_to_all x3, blocking collectives, exchanged(): lax.all_to_all(x, axis, 0, 0, axis_index_groups=[list(order)], tiled=True)  52.1 us
    pallas_call x1, Pallas kernels, per_device(): pl.pallas_call(pairs_kernel, out_shape=pltpu.VMEM((members, 1, LANES), f3...  4.83 us

profile of v10, /device:TPU:1, one launch (start us, length us, event | category | flops | bytes accessed | tf_op | source)
XLA Modules:
  0.0 59.3 jit_solution(9098589859059284370)
XLA Ops:
  0.6 1.0 %pack.1 = f32[16,8,1024]{2,1,0:T(8,128)S(1)} custom-call(s32[1024]{0:T(1024)} %index_ref.1, f32[3,1024]{1,0:T(4,128)} %pos_ref.1, f32[3,1024]{1,0:T(4,128)} %vel_ref.1, f32[1,1024]{1,0:T(1,128)} %bitcast.3), custom_call_target="tpu_custom_call" | custom-call | tf_op jit(solution)/shard_map/pack/pallas_call | solution.py:187
  1.7 12.8 %all_to_all.15.in_ref.field_ref = f32[16,8,1024]{2,1,0:T(8,128)S(1)} all-to-all(f32[16,8,1024]{2,1,0:T(8,128)S(1)} %pack.1), channel_id=1, replica_groups={{320,0,384,96,256,64,448,192,352,480,224,128,288,416,32,160},{321,1,385..., dimensions={0} | all-to-all | bytes 1048576 | tf_op jit(solution)/shard_map/all_to_all | solution.py:32
  14.5 25.3 %all_to_all.16.state_ref = f32[32,3,1,128]{3,2,1,0:T(1,128)S(1)} all-to-all(f32[32,3,1,128]{3,2,1,0:T(1,128)S(1)} %spread.1), channel_id=1, replica_groups={{17,1,0,16,3,2,31,30,5,4,29,28,7,6,27,26,9,8,25,24,11,10,23,22,13,12,21..., dimensions={0} | all-to-all | bytes 98304 | tf_op jit(solution)/shard_map/all_to_all | solution.py:32
  39.9 4.8 %pairs.1 = f32[32,1,128]{2,1,0:T(1,128)S(1)} custom-call(f32[32,3,1,128]{3,2,1,0:T(1,128)S(1)} %all_to_all.16.state_ref, f32[16,8,1024]{2,1,0:T(8,128)S(1)} %all_to_all.15.in_ref.field_ref), custom_call_target="tpu_custom_call" | custom-call | tf_op jit(solution)/shard_map/pairs/pallas_call | solution.py:204
  44.7 14.0 %all_to_all.17.refs_0_ = f32[32,1,128]{2,1,0:T(1,128)S(1)} all-to-all(f32[32,1,128]{2,1,0:T(1,128)S(1)} %pairs.1), channel_id=1, replica_groups={{17,1,0,16,3,2,31,30,5,4,29,28,7,6,27,26,9,8,25,24,11,10,23,22,13,12,21..., dimensions={0} | all-to-all | bytes 32768 | tf_op jit(solution)/shard_map/all_to_all | solution.py:32
  58.7 0.7 %finish.1 = (f32[2,3]{1,0:T(2,128)}, f32[2,3]{1,0:T(2,128)}) custom-call(f32[32,1,128]{2,1,0:T(1,128)S(1)} %all_to_all.17.refs_0_), custom_call_target="tpu_custom_call" | custom-call | tf_op jit(solution)/shard_map/finish/pallas_call | solution.py:215
  (1 shorter events, 0.0 us)
